TPU v7x, 32 devices: a whole 2x2x4 slice. The times are simulated.
32 devices in a mesh: band: 8 (over z, y), slab: 4 (over x, core).
Axes of the slice: x: 2, y: 2, z: 4, core: 2. Of those that a mesh axis runs over, the one named last changes fastest.
Arguments:
- bands: float32 [32, 32, 24, 128], P('band', 'slab'), may hold values from -8 to 8
- potential: float32 [32, 24, 128], P('slab'), may hold values from -1 to 0
Outputs:
- filtered: float32 [32, 32, 24, 128], P('band', 'slab')
- correlation: float32 [32, 32], P('band')
- projected: float32 [32, 32], P('band')
All inputs are finite; a program needn't handle non-finite values.
Results may differ from a plain program's by a relative error of at most 0.000092.
Values sent between devices are 32-bit elements; how exact they have to be, the bound alone decides.
A program may use at most 128 MiB of HBM per device.

v0:
```python
import jax
import jax.numpy as jnp
from jax import lax
from jax.sharding import PartitionSpec as P

centre = 4.5
half = 3.5


def extended(block, sides, width):
    for axis, dim in sides:
        count = lax.axis_size(axis)
        forward = [(i, i + 1) for i in range(count - 1)]
        forward.append((count - 1, 0))
        backward = [(target, source) for source, target in forward]
        low = lax.ppermute(
            lax.slice_in_dim(block, block.shape[dim] - width, None, axis=dim), axis, forward
        )
        high = lax.ppermute(lax.slice_in_dim(block, 0, width, axis=dim), axis, backward)
        block = jnp.concatenate([low, block, high], axis=dim)
    return block


def hamiltonian(field, potential):
    padded = extended(field, (("slab", 1),), 2)
    middle = padded[:, 2:-2]
    lap = (
        -2.5 * middle
        + 4.0 / 3.0 * (padded[:, 1:-3] + padded[:, 3:-1])
        - 1.0 / 12.0 * (padded[:, :-4] + padded[:, 4:])
    )
    for axis in (2, 3):
        lap = lap - 2.5 * middle
        lap = lap + 4.0 / 3.0 * (jnp.roll(middle, 1, axis) + jnp.roll(middle, -1, axis))
        lap = lap - 1.0 / 12.0 * (jnp.roll(middle, 2, axis) + jnp.roll(middle, -2, axis))
    return -0.5 * lap + potential[None] * middle


def body(bands, potential):
    previous = bands
    current = (hamiltonian(bands, potential) - centre * bands) / half
    for step in range(3):
        following = 2.0 * (hamiltonian(current, potential) - centre * current) / half - previous
        previous, current = (current, following)
    image = hamiltonian(current, potential)
    local_bands = current.shape[0]
    volume = 1.0 / (current.shape[1] * lax.axis_size("slab") * current.shape[2] * current.shape[3])
    flat = current.reshape(local_bands, -1)
    himage = image.reshape(local_bands, -1)
    cell_bands, cell_images = (
        lax.all_to_all(flat, "band", split_axis=1, concat_axis=0, tiled=True),
        lax.all_to_all(himage, "band", split_axis=1, concat_axis=0, tiled=True),
    )
    gram_full = jnp.dot(
        cell_bands,
        cell_bands.T,
        precision=lax.Precision.HIGHEST,
        preferred_element_type=jnp.float32,
    )
    proj_full = jnp.dot(
        cell_images,
        cell_bands.T,
        precision=lax.Precision.HIGHEST,
        preferred_element_type=jnp.float32,
    )
    gram_rows, proj_rows = (
        lax.psum_scatter(gram_full, "band", scatter_dimension=0, tiled=True),
        lax.psum_scatter(proj_full, "band", scatter_dimension=0, tiled=True),
    )
    gram_total, proj_total = lax.psum((gram_rows, proj_rows), "slab")
    return (current, gram_total * volume, proj_total * volume)


def solution(mesh):
    in_specs = (P("band", "slab", None, None), P("slab", None, None))
    out_specs = (P("band", "slab", None, None), P("band", None), P("band", None))
    return jax.shard_map(body, mesh=mesh, in_specs=in_specs, out_specs=out_specs, check_vma=False)
```

profile of v0, /device:TPU:0, one launch (start us, length us, event | category | flops | bytes accessed | tf_op | source)
XLA Modules:
  0.0 108.8 jit_solution(3802660535514599)
XLA Ops:
  0.6 1.0 fusion.143
  1.7 0.5 collective-permute-start
  2.2 2.0 %collective-permute-start.1 = (f32[4,2,24,128]{3,2,1,0:T(8,128)S(1)}, f32[4,2,24,128]{3,2,1,0:T(8,128)S(1)}, u32[]{:S(2)}, u32[]{:S(2)}) collective-permute-start(f32[4,2,24,128]{3,2,1,0:T(8,128)S(1)} %get-tuple-element.84), channel_id=1, source_target_pairs={{1,0},{2,1},{3,2},{0,3},{5,4},{6,5},{7,6},{4,7},{9,8},{10,9},{11,1... | collective-permute-start | bytes 294920 | tf_op jit(solution)/shard_map/ppermute | solution.py:19
  4.6 0.2 fusion.149
  4.8 0.2 fusion.150
  5.0 0.9 copy-done.2
  6.0 0.4 collective-permute-done
  6.5 0.8 collective-permute-done.1
  7.3 0.7 broadcast_multiply_fusion
  8.2 0.2 fusion.135
  8.4 0.2 fusion.136
  8.6 0.2 fusion.137
  8.9 1.6 %collective-permute-start.2 = (f32[4,2,24,128]{3,2,1,0:T(8,128)S(1)}, f32[4,2,24,128]{3,2,1,0:T(8,128)S(1)}, u32[]{:S(2)}, u32[]{:S(2)}) collective-permute-start(f32[4,2,24,128]{3,2,1,0:T(8,128)S(1)} %get-tuple-element.79), channel_id=1, source_target_pairs={{0,1},{1,2},{2,3},{3,0},{4,5},{5,6},{6,7},{7,4},{8,9},{9,10},{10,1... | collective-permute-start | bytes 294920 | tf_op jit(solution)/shard_map/ppermute | solution.py:16
  10.5 0.6 collective-permute-start.3
  11.2 2.2 %collective-permute-done.2 = f32[4,2,24,128]{3,2,1,0:T(8,128)S(1)} collective-permute-done((f32[4,2,24,128]{3,2,1,0:T(8,128)S(1)}, f32[4,2,24,128]{3,2,1,0:T(8,128)S(1)}, u32[]{:S(2)}, u32[]{:S(2)}) %collective-permute-start.2) | collective-permute-done | bytes 98336 | tf_op jit(solution)/shard_map/ppermute | solution.py:16
  13.4 0.7 collective-permute-done.3
  14.1 0.8 fusion.63
  15.8 1.6 %collective-permute-start.4 = (f32[4,2,24,128]{3,2,1,0:T(8,128)S(1)}, f32[4,2,24,128]{3,2,1,0:T(8,128)S(1)}, u32[]{:S(2)}, u32[]{:S(2)}) collective-permute-start(f32[4,2,24,128]{3,2,1,0:T(8,128)S(1)} %get-tuple-element.61), channel_id=1, source_target_pairs={{0,1},{1,2},{2,3},{3,0},{4,5},{5,6},{6,7},{7,4},{8,9},{9,10},{10,1... | collective-permute-start | bytes 294920 | tf_op jit(solution)/shard_map/ppermute | solution.py:16
  17.4 0.4 collective-permute-start.5
  17.8 2.2 %collective-permute-done.4 = f32[4,2,24,128]{3,2,1,0:T(8,128)S(1)} collective-permute-done((f32[4,2,24,128]{3,2,1,0:T(8,128)S(1)}, f32[4,2,24,128]{3,2,1,0:T(8,128)S(1)}, u32[]{:S(2)}, u32[]{:S(2)}) %collective-permute-start.4) | collective-permute-done | bytes 98336 | tf_op jit(solution)/shard_map/ppermute | solution.py:16
  20.1 0.6 collective-permute-done.5
  20.7 0.8 fusion.46
  22.3 1.6 %collective-permute-start.6 = (f32[4,2,24,128]{3,2,1,0:T(8,128)S(1)}, f32[4,2,24,128]{3,2,1,0:T(8,128)S(1)}, u32[]{:S(2)}, u32[]{:S(2)}) collective-permute-start(f32[4,2,24,128]{3,2,1,0:T(8,128)S(1)} %get-tuple-element.43), channel_id=1, source_target_pairs={{0,1},{1,2},{2,3},{3,0},{4,5},{5,6},{6,7},{7,4},{8,9},{9,10},{10,1... | collective-permute-start | bytes 294920 | tf_op jit(solution)/shard_map/ppermute | solution.py:16
  23.9 0.5 collective-permute-start.7
  24.4 2.2 %collective-permute-done.6 = f32[4,2,24,128]{3,2,1,0:T(8,128)S(1)} collective-permute-done((f32[4,2,24,128]{3,2,1,0:T(8,128)S(1)}, f32[4,2,24,128]{3,2,1,0:T(8,128)S(1)}, u32[]{:S(2)}, u32[]{:S(2)}) %collective-permute-start.6) | collective-permute-done | bytes 98336 | tf_op jit(solution)/shard_map/ppermute | solution.py:16
  26.6 0.6 collective-permute-done.7
  27.2 0.7 fusion.29
  28.5 1.0 fusion.110
  29.5 1.0 fusion.111
  30.5 1.0 fusion.113
  31.6 1.6 %collective-permute-start.8 = (f32[4,2,24,128]{3,2,1,0:T(8,128)S(1)}, f32[4,2,24,128]{3,2,1,0:T(8,128)S(1)}, u32[]{:S(2)}, u32[]{:S(2)}) collective-permute-start(f32[4,2,24,128]{3,2,1,0:T(8,128)S(1)} %get-tuple-element.25), channel_id=1, source_target_pairs={{0,1},{1,2},{2,3},{3,0},{4,5},{5,6},{6,7},{7,4},{8,9},{9,10},{10,1... | collective-permute-start | bytes 294920 | tf_op jit(solution)/shard_map/ppermute | solution.py:16
  33.1 0.5 collective-permute-start.9
  33.6 1.0 copy.7
  34.6 4.1 %all-to-all-start = ((f32[4,8,3072]{2,0,1:T(4,128)}), f32[4,8,3072]{2,0,1:T(4,128)S(1)}, u32[]{:S(2)}, u32[]{:S(2)}) async-start(f32[4,8,3072]{2,0,1:T(4,128)} %copy.7), calls=%async_computation | async-start | bytes 786432 | tf_op jit(solution)/shard_map/all_to_all | solution.py:51
  38.8 3.1 %fusion.12 = f32[4,8,24,128]{3,2,1,0:T(8,128)} fusion(f32[4,8,24,128]{3,2,1,0:T(8,128)S(1)} %fusion.29, f32[4,2,24,128]{3,2,1,0:T(8,128)} %collective-permute-done.9, f32[4,2,24,128]{3,2,1,0:T(8,128)S(1)} %collective-permute-done.8, f32[4,8,23,128]{3,2,1,0:T(8,128)} %get-tuple-element.22, f32[4,8,1,128]{3,2,1,0:T(1,128)S(1)} %get-tuple-element.24, ...), kind=kLoop, calls=%fused_computation.28 | loop fusion | flops 3637248 | bytes 4227072 | tf_op jit(solution)/shard_map/add | solution.py:36
  41.9 1.1 all_to_all.32
  43.0 1.0 copy.8
  44.0 6.6 %all-to-all-done = f32[4,8,3072]{2,0,1:T(4,128)S(1)} async-done(((f32[4,8,3072]{2,0,1:T(4,128)}), f32[4,8,3072]{2,0,1:T(4,128)S(1)}, u32[]{:S(2)}, u32[]{:S(2)}) %all-to-all-start) | async-done | bytes 393248 | tf_op jit(solution)/shard_map/all_to_all | solution.py:51
  50.6 3.6 %all-to-all-start.1 = ((f32[4,8,3072]{2,0,1:T(4,128)}), f32[4,8,3072]{2,0,1:T(4,128)S(1)}, u32[]{:S(2)}, u32[]{:S(2)}) async-start(f32[4,8,3072]{2,0,1:T(4,128)} %copy.8), calls=%async_computation.1 | async-start | bytes 786432 | tf_op jit(solution)/shard_map/all_to_all | solution.py:52
  54.3 0.7 copy-done.3
  54.9 0.6 dynamic-slice
  56.3 0.5 fusion.152
  56.8 9.3 %all-to-all-done.1 = f32[4,8,3072]{2,0,1:T(4,128)S(1)} async-done(((f32[4,8,3072]{2,0,1:T(4,128)}), f32[4,8,3072]{2,0,1:T(4,128)S(1)}, u32[]{:S(2)}, u32[]{:S(2)}) %all-to-all-start.1) | async-done | bytes 393248 | tf_op jit(solution)/shard_map/all_to_all | solution.py:52
  66.2 0.4 fusion.153
  66.7 35.2 %all-reduce.2 = (f32[32,32]{1,0:T(8,128)S(1)}, f32[32,32]{1,0:T(8,128)S(1)}) all-reduce(f32[32,32]{1,0:T(8,128)S(1)} %fusion.152, f32[32,32]{1,0:T(8,128)S(1)} %fusion.153), channel_id=2, replica_groups=mesh['band'=8,'slab'=4] {'band'}, use_global_device_ids=true, to_apply=%region_0.1.clone | all-reduce | flops 2048 | bytes 16384
  101.9 5.8 %all-reduce.3 = (f32[4,32]{1,0:T(4,128)S(1)}, f32[4,32]{1,0:T(4,128)S(1)}) all-reduce(f32[4,32]{1,0:T(4,128)S(1)} %get-tuple-element.102, f32[4,32]{1,0:T(4,128)S(1)} %get-tuple-element.101), channel_id=1, replica_groups=mesh['band'=8,'slab'=4] {'slab'}, use_global_device_ids=true, to_apply=%region_1.2 | all-reduce | flops 256 | bytes 2048 | tf_op jit(solution)/shard_map/psum | solution.py:70
  107.7 0.6 broadcast_multiply_fusion.2
  108.3 0.6 broadcast_multiply_fusion.3
  (52 shorter events, 3.8 us)
Async XLA Ops:
  0.6 3.5 %copy-start.1 = (f32[4,8,24,128]{3,2,1,0:T(8,128)S(1)}, f32[4,8,24,128]{3,2,1,0:T(8,128)}, u32[]{:S(2)}) copy-start(f32[4,8,24,128]{3,2,1,0:T(8,128)} %param.2) | copy-start | bytes 1179652
  1.7 4.7 %collective-permute-start = (f32[4,2,24,128]{3,2,1,0:T(8,128)S(1)}, f32[4,2,24,128]{3,2,1,0:T(8,128)S(1)}, u32[]{:S(2)}, u32[]{:S(2)}) collective-permute-start(f32[4,2,24,128]{3,2,1,0:T(8,128)S(1)} %get-tuple-element.83), channel_id=1, source_target_pairs={{0,1},{1,2},{2,3},{3,0},{4,5},{5,6},{6,7},{7,4},{8,9},{9,10},{10,1... | collective-permute-start | bytes 294920 | tf_op jit(solution)/shard_map/ppermute | solution.py:16
  2.2 5.1 %collective-permute-start.1 = (f32[4,2,24,128]{3,2,1,0:T(8,128)S(1)}, f32[4,2,24,128]{3,2,1,0:T(8,128)S(1)}, u32[]{:S(2)}, u32[]{:S(2)}) collective-permute-start(f32[4,2,24,128]{3,2,1,0:T(8,128)S(1)} %get-tuple-element.84), channel_id=1, source_target_pairs={{1,0},{2,1},{3,2},{0,3},{5,4},{6,5},{7,6},{4,7},{9,8},{10,9},{11,1... | collective-permute-start | bytes 294920 | tf_op jit(solution)/shard_map/ppermute | solution.py:19
  5.0 0.9 copy-start.2
  8.9 4.5 %collective-permute-start.2 = (f32[4,2,24,128]{3,2,1,0:T(8,128)S(1)}, f32[4,2,24,128]{3,2,1,0:T(8,128)S(1)}, u32[]{:S(2)}, u32[]{:S(2)}) collective-permute-start(f32[4,2,24,128]{3,2,1,0:T(8,128)S(1)} %get-tuple-element.79), channel_id=1, source_target_pairs={{0,1},{1,2},{2,3},{3,0},{4,5},{5,6},{6,7},{7,4},{8,9},{9,10},{10,1... | collective-permute-start | bytes 294920 | tf_op jit(solution)/shard_map/ppermute | solution.py:16
  10.5 3.6 %collective-permute-start.3 = (f32[4,2,24,128]{3,2,1,0:T(8,128)S(1)}, f32[4,2,24,128]{3,2,1,0:T(8,128)S(1)}, u32[]{:S(2)}, u32[]{:S(2)}) collective-permute-start(f32[4,2,24,128]{3,2,1,0:T(8,128)S(1)} %get-tuple-element.80), channel_id=1, source_target_pairs={{1,0},{2,1},{3,2},{0,3},{5,4},{6,5},{7,6},{4,7},{9,8},{10,9},{11,1... | collective-permute-start | bytes 294920 | tf_op jit(solution)/shard_map/ppermute | solution.py:19
  15.8 4.3 %collective-permute-start.4 = (f32[4,2,24,128]{3,2,1,0:T(8,128)S(1)}, f32[4,2,24,128]{3,2,1,0:T(8,128)S(1)}, u32[]{:S(2)}, u32[]{:S(2)}) collective-permute-start(f32[4,2,24,128]{3,2,1,0:T(8,128)S(1)} %get-tuple-element.61), channel_id=1, source_target_pairs={{0,1},{1,2},{2,3},{3,0},{4,5},{5,6},{6,7},{7,4},{8,9},{9,10},{10,1... | collective-permute-start | bytes 294920 | tf_op jit(solution)/shard_map/ppermute | solution.py:16
  17.4 3.3 %collective-permute-start.5 = (f32[4,2,24,128]{3,2,1,0:T(8,128)S(1)}, f32[4,2,24,128]{3,2,1,0:T(8,128)S(1)}, u32[]{:S(2)}, u32[]{:S(2)}) collective-permute-start(f32[4,2,24,128]{3,2,1,0:T(8,128)S(1)} %get-tuple-element.62), channel_id=1, source_target_pairs={{1,0},{2,1},{3,2},{0,3},{5,4},{6,5},{7,6},{4,7},{9,8},{10,9},{11,1... | collective-permute-start | bytes 294920 | tf_op jit(solution)/shard_map/ppermute | solution.py:19
  22.3 4.3 %collective-permute-start.6 = (f32[4,2,24,128]{3,2,1,0:T(8,128)S(1)}, f32[4,2,24,128]{3,2,1,0:T(8,128)S(1)}, u32[]{:S(2)}, u32[]{:S(2)}) collective-permute-start(f32[4,2,24,128]{3,2,1,0:T(8,128)S(1)} %get-tuple-element.43), channel_id=1, source_target_pairs={{0,1},{1,2},{2,3},{3,0},{4,5},{5,6},{6,7},{7,4},{8,9},{9,10},{10,1... | collective-permute-start | bytes 294920 | tf_op jit(solution)/shard_map/ppermute | solution.py:16
  23.9 3.3 %collective-permute-start.7 = (f32[4,2,24,128]{3,2,1,0:T(8,128)S(1)}, f32[4,2,24,128]{3,2,1,0:T(8,128)S(1)}, u32[]{:S(2)}, u32[]{:S(2)}) collective-permute-start(f32[4,2,24,128]{3,2,1,0:T(8,128)S(1)} %get-tuple-element.44), channel_id=1, source_target_pairs={{1,0},{2,1},{3,2},{0,3},{5,4},{6,5},{7,6},{4,7},{9,8},{10,9},{11,1... | collective-permute-start | bytes 294920 | tf_op jit(solution)/shard_map/ppermute | solution.py:19
  28.0 10.8 %copy-start = (f32[4,8,24,128]{3,2,1,0:T(8,128)}, f32[4,8,24,128]{3,2,1,0:T(8,128)S(1)}, u32[]{:S(2)}) copy-start(f32[4,8,24,128]{3,2,1,0:T(8,128)S(1)} %fusion.29) | copy-start | bytes 1179652
  31.6 7.2 %collective-permute-start.8 = (f32[4,2,24,128]{3,2,1,0:T(8,128)S(1)}, f32[4,2,24,128]{3,2,1,0:T(8,128)S(1)}, u32[]{:S(2)}, u32[]{:S(2)}) collective-permute-start(f32[4,2,24,128]{3,2,1,0:T(8,128)S(1)} %get-tuple-element.25), channel_id=1, source_target_pairs={{0,1},{1,2},{2,3},{3,0},{4,5},{5,6},{6,7},{7,4},{8,9},{9,10},{10,1... | collective-permute-start | bytes 294920 | tf_op jit(solution)/shard_map/ppermute | solution.py:16
  33.1 5.6 %collective-permute-start.9 = (f32[4,2,24,128]{3,2,1,0:T(8,128)S(1)}, f32[4,2,24,128]{3,2,1,0:T(8,128)}, u32[]{:S(2)}, u32[]{:S(2)}) collective-permute-start(f32[4,2,24,128]{3,2,1,0:T(8,128)S(1)} %get-tuple-element.26), channel_id=1, source_target_pairs={{1,0},{2,1},{3,2},{0,3},{5,4},{6,5},{7,6},{4,7},{9,8},{10,9},{11,1... | collective-permute-start | bytes 294920 | tf_op jit(solution)/shard_map/ppermute | solution.py:19
  34.6 16.0 %all-to-all-start = ((f32[4,8,3072]{2,0,1:T(4,128)}), f32[4,8,3072]{2,0,1:T(4,128)S(1)}, u32[]{:S(2)}, u32[]{:S(2)}) async-start(f32[4,8,3072]{2,0,1:T(4,128)} %copy.7), calls=%async_computation | async-start | bytes 786432 | tf_op jit(solution)/shard_map/all_to_all | solution.py:51
  50.6 15.5 %all-to-all-start.1 = ((f32[4,8,3072]{2,0,1:T(4,128)}), f32[4,8,3072]{2,0,1:T(4,128)S(1)}, u32[]{:S(2)}, u32[]{:S(2)}) async-start(f32[4,8,3072]{2,0,1:T(4,128)} %copy.8), calls=%async_computation.1 | async-start | bytes 786432 | tf_op jit(solution)/shard_map/all_to_all | solution.py:52
  54.3 0.7 copy-start.3
where the time goes:
time: 109 us
  blocking collectives  41 us (38%)
  waiting for transfers between devices  25.7 us (24%)
  starting transfers between devices  18.6 us (17%)
  local copies, waits for them, and re-layouts  13.8 us (13%)
  other arithmetic  7.31 us (7%)
  between operations  1.56 us (1%)
    unnamed x1, blocking collectives  35.2 us
    all_to_all x1, waiting for transfers between devices, body(): lax.all_to_all(himage, 'band', split_axis=1, concat_axis=0, tiled=True)  9.34 us
    ppermute x5, waiting for transfers between devices, extended(): lax.ppermute(lax.slice_in_dim(block, block.shape[dim] - width, None, axis...  7.06 us
    ppermute x5, starting transfers between devices, extended(): lax.ppermute(lax.slice_in_dim(block, block.shape[dim] - width, None, axis...  6.89 us
    all_to_all x1, waiting for transfers between devices, body(): lax.all_to_all(flat, 'band', split_axis=1, concat_axis=0, tiled=True)  6.62 us
    psum x1, blocking collectives, body(): gram_total, proj_total = lax.psum((gram_rows, proj_rows), 'slab')  5.76 us
    all_to_all x1, starting transfers between devices, body(): lax.all_to_all(flat, 'band', split_axis=1, concat_axis=0, tiled=True)  4.08 us
    ppermute x5, starting transfers between devices, extended(): lax.ppermute(lax.slice_in_dim(block, 0, width, axis=dim), axis, backward)  3.99 us
  transfers between devices with their start and end apart: 12, of which 10 were waited for; matrix products, arithmetic and copies ran while one was open for 7% of the time, Pallas kernels for 0%

commit v1 on v0

v1 whole, which is shorter than its diff:
```python
import functools

import jax
import jax.numpy as jnp
from jax import lax
from jax.experimental import pallas as pl
from jax.experimental.pallas import tpu as pltpu
from jax.sharding import PartitionSpec as P

centre = 4.5
half = 3.5
MESH = pl.DeviceIdType.MESH
STEPS = 4


def shifted(v, axis):
    n = v.shape[axis]
    near = pltpu.roll(v, 1, axis) + pltpu.roll(v, n - 1, axis)
    far = pltpu.roll(v, 2, axis) + pltpu.roll(v, n - 2, axis)
    return near, far


def kernel(
    dims, bands, pot, f_out, c_out, p_out,
    e, vbuf, img, fall, iall, part, rb, rs,
    halo_send, halo_recv, load_sem, out_sem, gram_send, gram_recv,
    row_send, row_recv, slab_send, slab_recv,
):
    nb, ns, L, nz, ny, chunk, active, volume = dims
    b, s = lax.axis_index("band"), lax.axis_index("slab")
    up, down = lax.rem(s + 1, ns), lax.rem(s + ns - 1, ns)
    inner = pl.ds(2 * ny, nz * ny)

    load = pltpu.make_async_copy(bands, e.at[0, :, inner], load_sem.at[0])
    load.start()
    load_pot = pltpu.make_async_copy(pot, vbuf, load_sem.at[1])
    load_pot.start()

    barrier = pltpu.get_barrier_semaphore()

    def greet_band(d, carry):
        pl.semaphore_signal(
            barrier, inc=1, device_id={"band": lax.rem(b + d, nb)}, device_id_type=MESH
        )
        return carry

    lax.fori_loop(1, nb, greet_band, 0)
    for d in range(1, ns):
        pl.semaphore_signal(
            barrier, inc=1, device_id={"slab": lax.rem(s + d, ns)}, device_id_type=MESH
        )
    pl.semaphore_wait(barrier, nb - 1 + ns - 1)

    def halo(k):
        if k == 0:
            low, high = bands.at[:, pl.ds(0, 2 * ny)], bands.at[:, pl.ds((nz - 2) * ny, 2 * ny)]
        else:
            low, high = e.at[k, :, pl.ds(2 * ny, 2 * ny)], e.at[k, :, pl.ds(nz * ny, 2 * ny)]
        return (
            pltpu.make_async_remote_copy(
                src_ref=low,
                dst_ref=e.at[k, :, pl.ds((nz + 2) * ny, 2 * ny)],
                send_sem=halo_send.at[k, 0],
                recv_sem=halo_recv.at[k, 0],
                device_id={"slab": down},
                device_id_type=MESH,
            ),
            pltpu.make_async_remote_copy(
                src_ref=high,
                dst_ref=e.at[k, :, pl.ds(0, 2 * ny)],
                send_sem=halo_send.at[k, 1],
                recv_sem=halo_recv.at[k, 1],
                device_id={"slab": up},
                device_id_type=MESH,
            ),
        )

    def plane(k, z):
        def rows(offset):
            return pl.ds(pl.multiple_of((z + 2 + offset) * ny, 8), ny)

        here = pl.ds(pl.multiple_of(z * ny, 8), ny)
        scale = 1.0 if k == STEPS else (1.0 if k == 0 else 2.0) / half
        shift = 3.75 if k == STEPS else 3.75 - centre
        diagonal = (vbuf[here, :] + shift) * scale
        for l in range(L):
            v = e[k, l, rows(0), :]
            near = e[k, l, rows(-1), :] + e[k, l, rows(1), :]
            far = e[k, l, rows(-2), :] + e[k, l, rows(2), :]
            for axis in (0, 1):
                n1, n2 = shifted(v, axis)
                near = near + n1
                far = far + n2
            value = diagonal * v - (scale * 2.0 / 3.0) * near + (scale / 24.0) * far
            if k == STEPS:
                img[l, here, :] = value
            else:
                if k > 0:
                    value = value - e[k - 1, l, rows(0), :]
                e[k + 1, l, rows(0), :] = value

    def planes(k, start, stop):
        def step(z, carry):
            plane(k, z)
            return carry

        lax.fori_loop(start, stop, step, 0)

    def regroup(which, d, back=False):
        peer = lax.rem(b + d, nb)
        cells = pl.multiple_of(peer * chunk, 8)
        if which == 0:
            src = e.at[STEPS, :, pl.ds(2 * ny + cells, chunk)]
        else:
            src = img.at[:, pl.ds(cells, chunk)]
        return pltpu.make_async_remote_copy(
            src_ref=src,
            dst_ref=(fall, iall)[which].at[b],
            send_sem=gram_send.at[which, d],
            recv_sem=gram_recv.at[which, d],
            device_id={"band": peer},
            device_id_type=MESH,
        ), peer

    def regroup_start(which):
        def step(d, carry):
            copy, peer = regroup(which, d)
            if active == nb:
                copy.start()
            else:
                @pl.when(peer < active)
                def _():
                    copy.start()
            return carry

        lax.fori_loop(1, nb, step, 0)

    def regroup_own(which):
        mine = pl.multiple_of(b * chunk, 8)
        if which == 0:
            fall[b] = e[STEPS, :, pl.ds(2 * ny + mine, chunk), :]
        else:
            iall[b] = img[:, pl.ds(mine, chunk), :]

    def regroup_arrive(which):
        def step(d, carry):
            copy, _ = regroup(which, d)
            copy.wait_recv()
            return carry

        lax.fori_loop(1, nb, step, 0)

    def regroup_sent(which):
        def step(d, carry):
            copy, peer = regroup(which, d)
            if active == nb:
                copy.wait_send()
            else:
                @pl.when(peer < active)
                def _():
                    copy.wait_send()
            return carry

        lax.fori_loop(1, nb, step, 0)

    def cells_of(ref):
        flat = ref.reshape(nb * L * chunk, ref.shape[-1])
        return jnp.concatenate(
            [flat[pl.ds(r, nb * L, stride=chunk), :] for r in range(chunk)], axis=1
        )

    def product(x, y):
        return lax.dot_general(
            x, y, (((1,), (1,)), ((), ())),
            precision=lax.Precision.HIGHEST, preferred_element_type=jnp.float32,
        )

    def working(action):
        if active == nb:
            action()
        else:
            pl.when(b < active)(action)

    for copy in halo(0):
        copy.start()
    load.wait()
    load_pot.wait()
    for k in range(STEPS):
        if k == 0:
            planes(0, 2, nz - 2)
        for copy in halo(k):
            copy.wait_recv()
        planes(k, 0, 2)
        planes(k, nz - 2, nz)
        for copy in halo(k + 1):
            copy.start()
        if k > 0:
            planes(k, 2, nz - 2)
    regroup_start(0)
    result = pltpu.make_async_copy(e.at[STEPS, :, inner], f_out, out_sem)
    result.start()
    planes(STEPS, 2, nz - 2)
    for copy in halo(STEPS):
        copy.wait_recv()
    planes(STEPS, 0, 2)
    planes(STEPS, nz - 2, nz)
    regroup_start(1)

    def correlate():
        regroup_own(0)
        regroup_own(1)
        regroup_arrive(0)
        fs = cells_of(fall)
        gram = product(fs, fs) * volume
        for g in range(nb):
            part[g, 0:L, :] = gram[g * L:(g + 1) * L]
        regroup_arrive(1)
        proj = product(cells_of(iall), cells_of(fall)) * volume
        for g in range(nb):
            part[g, L:2 * L, :] = proj[g * L:(g + 1) * L]

    working(correlate)
    if active != nb:
        @pl.when(b >= active)
        def _():
            part[...] = jnp.zeros_like(part)

    def row(d):
        peer = lax.rem(b + d, nb)
        return pltpu.make_async_remote_copy(
            src_ref=part.at[peer],
            dst_ref=rb.at[b],
            send_sem=row_send.at[d],
            recv_sem=row_recv.at[d],
            device_id={"band": peer},
            device_id_type=MESH,
        )

    def each_row(action):
        def step(d, carry):
            action(row(d))
            return carry

        lax.fori_loop(1, nb, step, 0)

    each_row(lambda copy: copy.start())
    rb[b] = part[b]
    each_row(lambda copy: copy.wait_recv())
    rs[s] = jnp.sum(rb[...], axis=0)

    def across(d):
        return pltpu.make_async_remote_copy(
            src_ref=rs.at[s],
            dst_ref=rs.at[s],
            send_sem=slab_send.at[d],
            recv_sem=slab_recv.at[d],
            device_id={"slab": lax.rem(s + d, ns)},
            device_id_type=MESH,
        )

    for d in range(1, ns):
        across(d).start()
    for d in range(1, ns):
        across(d).wait_recv()
    total = rs[0]
    for other in range(1, ns):
        total = total + rs[other]
    c_out[...] = total[:L]
    p_out[...] = total[L:]
    for d in range(1, ns):
        across(d).wait_send()
    each_row(lambda copy: copy.wait_send())
    for k in range(STEPS + 1):
        for copy in halo(k):
            copy.wait_send()
    regroup_sent(0)
    regroup_sent(1)
    result.wait()


def body(bands, potential):
    L, nz, ny, nx = bands.shape
    nb, ns = lax.axis_size("band"), lax.axis_size("slab")
    rows = nz * ny
    tiles = rows // 8
    each = -(-tiles // nb)
    while tiles % each:
        each += 1
    chunk = each * 8
    active = rows // chunk
    dims = (nb, ns, L, nz, ny, chunk, active, 1.0 / (rows * ns * nx))
    f32 = jnp.float32
    anywhere, vmem = pl.BlockSpec(memory_space=pl.ANY), pl.BlockSpec(memory_space=pltpu.VMEM)
    dma = pltpu.SemaphoreType.DMA
    f, c, p = pl.pallas_call(
        functools.partial(kernel, dims),
        out_shape=(
            jax.ShapeDtypeStruct((L, rows, nx), f32),
            jax.ShapeDtypeStruct((L, nb * L), f32),
            jax.ShapeDtypeStruct((L, nb * L), f32),
        ),
        in_specs=[anywhere, anywhere],
        out_specs=(anywhere, vmem, vmem),
        scratch_shapes=[
            pltpu.VMEM((STEPS + 1, L, (nz + 4) * ny, nx), f32),
            pltpu.VMEM((rows, nx), f32),
            pltpu.VMEM((L, rows, nx), f32),
            pltpu.VMEM((nb, L, chunk, nx), f32),
            pltpu.VMEM((nb, L, chunk, nx), f32),
            pltpu.VMEM((nb, 2 * L, nb * L), f32),
            pltpu.VMEM((nb, 2 * L, nb * L), f32),
            pltpu.VMEM((ns, 2 * L, nb * L), f32),
            dma((STEPS + 1, 2)), dma((STEPS + 1, 2)),
            dma((2,)), dma,
            dma((2, nb)), dma((2, nb)),
            dma((nb,)), dma((nb,)),
            dma((ns,)), dma((ns,)),
        ],
        compiler_params=pltpu.CompilerParams(
            collective_id=0, has_side_effects=True, vmem_limit_bytes=40 * 1024 * 1024
        ),
    )(bands.reshape(L, rows, nx), potential.reshape(rows, nx))
    return f.reshape(L, nz, ny, nx), c, p


def solution(mesh):
    in_specs = (P("band", "slab", None, None), P("slab", None, None))
    out_specs = (P("band", "slab", None, None), P("band", None), P("band", None))
    return jax.shard_map(body, mesh=mesh, in_specs=in_specs, out_specs=out_specs, check_vma=False)
```

time: 109 us -> 55.9 us (0.51)
  Pallas kernels: 0 us -> 51.3 us
  blocking collectives: 41 us -> 0 us
  waiting for transfers between devices: 25.7 us -> 0 us
  starting transfers between devices: 18.6 us -> 0 us
  local copies, waits for them, and re-layouts: 13.8 us -> 3.78 us
  other arithmetic: 7.31 us -> 0 us
    pallas_call x0 -> x1, Pallas kernels: none -> 51.3 us  [body(): pl.pallas_call(functools.partial(kernel, dims), out_shape=(jax.ShapeDtype...]
    unnamed x1 -> x0, blocking collectives: 35.2 us -> none
    all_to_all x2 -> x0, waiting for transfers between devices: 16 us -> none  [the longest x1 9.34 us: body(): lax.all_to_all(himage, 'band', split_axis=1, concat_axis=0, tiled=True)]
    ppermute x10 -> x0, starting transfers between devices: 10.9 us -> none  [the longest x5 6.89 us: extended(): lax.ppermute(lax.slice_in_dim(block, block.shape[dim] - width, None, axis...]
    ppermute x10 -> x0, waiting for transfers between devices: 9.74 us -> none  [the longest x5 7.06 us: extended(): lax.ppermute(lax.slice_in_dim(block, block.shape[dim] - width, None, axis...]
    slice x45 -> x0, local copies, waits for them, and re-layouts: 8.17 us -> none  [the longest x16 3.53 us: hamiltonian(): jnp.roll(middle, -1, axis)]
    all_to_all x2 -> x0, starting transfers between devices: 7.72 us -> none  [the longest x1 4.08 us: body(): lax.all_to_all(flat, 'band', split_axis=1, concat_axis=0, tiled=True)]
    psum x1 -> x0, blocking collectives: 5.76 us -> none  [body(): gram_total, proj_total = lax.psum((gram_rows, proj_rows), 'slab')]
  transfers between devices with their start and end apart: 12 -> 0, of which waited for: 10 -> 0; matrix products, arithmetic and copies ran while one was open for 7% -> 0% of each run, Pallas kernels for 0% -> 0%
where the time goes in v1:
time: 55.9 us; the launch traced here: 55.7 us
  Pallas kernels  51.3 us (92%)
  local copies, waits for them, and re-layouts  3.78 us (7%)
  between operations  0.65 us (1%)
    pallas_call x1, Pallas kernels, body(): pl.pallas_call(functools.partial(kernel, dims), out_shape=(jax.ShapeDtype...  51.3 us
    unnamed x7, local copies, waits for them, and re-layouts  3.78 us

profile of v1, /device:TPU:0, one launch (start us, length us, event | category | flops | bytes accessed | tf_op | source)
XLA Modules:
  0.0 55.7 jit_solution(5656227136716539753)
XLA Ops:
  0.6 0.0 copy-start
  0.6 1.0 %copy-done = f32[4,8,24,128]{3,2,1,0:T(8,128)S(1)} copy-done((f32[4,8,24,128]{3,2,1,0:T(8,128)S(1)}, f32[4,8,24,128]{3,2,1,0:T(8,128)}, u32[]{:S(2)}) %copy-start) | copy-done | bytes 393240
  1.6 0.0 copy-start.1
  1.6 0.9 %copy-done.1 = f32[8,24,128]{2,1,0:T(8,128)S(1)} copy-done((f32[8,24,128]{2,1,0:T(8,128)S(1)}, f32[8,24,128]{2,1,0:T(8,128)}, u32[]{:S(2)}) %copy-start.1) | copy-done | bytes 98328
  2.5 51.3 %shard_map.49 = (f32[4,192,128]{2,1,0:T(8,128)S(1)}, f32[4,32]{1,0:T(4,128)S(1)}, f32[4,32]{1,0:T(4,128)S(1)}) custom-call(f32[4,192,128]{2,1,0:T(8,128)S(1)} %bitcast.4, f32[192,128]{1,0:T(8,128)S(1)} %bitcast.5), custom_call_target="tpu_custom_call" | custom-call | tf_op jit(solution)/shard_map/pallas_call | solution.py:295
  53.8 0.7 %copy.8 = f32[4,8,24,128]{3,2,1,0:T(8,128)} copy(f32[4,8,24,128]{3,2,1,0:T(8,128)S(1)} %bitcast.3) | data formatting | bytes 786432
  54.6 0.6 %copy.9 = f32[4,32]{1,0:T(4,128)} copy(f32[4,32]{1,0:T(4,128)S(1)} %get-tuple-element.13) | data formatting | bytes 1024
  55.2 0.6 %copy.10 = f32[4,32]{1,0:T(4,128)} copy(f32[4,32]{1,0:T(4,128)S(1)} %get-tuple-element.14) | data formatting | bytes 1024
Async XLA Ops:
  0.6 1.0 %copy-start = (f32[4,8,24,128]{3,2,1,0:T(8,128)S(1)}, f32[4,8,24,128]{3,2,1,0:T(8,128)}, u32[]{:S(2)}) copy-start(f32[4,8,24,128]{3,2,1,0:T(8,128)} %param.2) | copy-start | bytes 1179652
  1.6 0.9 %copy-start.1 = (f32[8,24,128]{2,1,0:T(8,128)S(1)}, f32[8,24,128]{2,1,0:T(8,128)}, u32[]{:S(2)}) copy-start(f32[8,24,128]{2,1,0:T(8,128)} %param.3) | copy-start | bytes 294916
